TPU v7x, 32 devices: a whole 2x2x4 slice. The times are simulated.
32 devices in a mesh: gx: 4 (over z), gy: 4 (over y, x), gz: 2 (over core).
Axes of the slice: x: 2, y: 2, z: 4, core: 2. Of those that a mesh axis runs over, the one named last changes fastest.
Arguments:
- field: float32 [4, 256, 128, 1024], P(None, 'gx', 'gz', 'gy'), may hold values from -6 to 6
- basis_two: float32 [1024, 64], P('gy'), may hold values from -0.1875 to 0.1875
- basis_three: float32 [128, 64], P('gz'), may hold values from -0.5 to 0.5
Outputs:
- projected: float32 [256, 16384], P('gx', ('gy', 'gz'))
- gram: float32 [256, 256], P('gx')
All inputs are finite; a program needn't handle non-finite values.
Results may differ from a plain program's by a relative error of at most 0.000071.
Values sent between devices are 32-bit elements; how exact they have to be, the bound alone decides.
A program may use at most 128 MiB of HBM per device.

v0:
```python
import jax
import jax.numpy as jnp
from jax import lax
from jax.sharding import PartitionSpec as P

V = 4
R = 64


def body(field, basis_two, basis_three):
    highest = lax.Precision.HIGHEST
    rows = field.shape[1]
    first = jnp.einsum("vacb,bs->vacs", field, basis_two, precision=highest)
    core = jnp.einsum("vacs,ct->avst", first, basis_three, precision=highest)
    core = core.reshape(rows, -1)
    projected = lax.psum_scatter(core, ("gy", "gz"), scatter_dimension=1, tiled=True)
    partial_gram = jnp.dot(
        projected,
        lax.all_gather(projected, "gx", axis=0, tiled=True).T,
        precision=highest,
        preferred_element_type=jnp.float32,
    )
    gram = lax.psum(partial_gram, ("gy", "gz")) / jnp.float32(V * R * R)
    return (projected, gram)


def solution(mesh):
    placed = (P(None, "gx", "gz", "gy"), P("gy", None), P("gz", None))
    return jax.shard_map(
        body,
        mesh=mesh,
        in_specs=placed,
        out_specs=(P("gx", ("gy", "gz")), P("gx", None)),
        check_vma=False,
    )
```

profile of v0, /device:TPU:0, one launch (start us, length us, event | category | flops | bytes accessed | tf_op | source)
XLA Modules:
  0.0 219.7 jit_solution(12850653019481287499)
XLA Ops:
  7.2 0.0 copy-start
  7.2 0.0 copy-start.1
  7.2 0.0 reduce-scatter.2.cloned.1.call-start
  7.2 0.8 copy-done
  8.0 26.7 %fusion = f32[4,64,64,64]{2,3,1,0:T(8,128)S(1)} fusion(f32[4,64,64,256]{3,2,1,0:T(8,128)} %param.3, f32[256,64]{0,1:T(8,128)S(1)} %copy-done), kind=kOutput, calls=%fused_computation.1 | convolution fusion | flops 3221225472 | bytes 21037056 | tf_op jit(solution)/shard_map/vacb,bs->vacs/dot_general | solution.py:13
  34.7 0.0 copy-done.1
  34.7 7.8 %convolution_bitcast_fusion = f32[64,4,64,64]{3,2,0,1:T(8,128)S(1)} fusion(f32[4,64,64,64]{2,3,1,0:T(8,128)S(1)} %fusion, f32[64,64]{1,0:T(8,128)S(1)} %copy-done.1), kind=kOutput, calls=%fused_computation | convolution fusion | flops 805306368 | bytes 8404992 | tf_op jit(solution)/shard_map/vacs,ct->avst/dot_general | solution.py:14
  42.5 4.1 %copy.5 = f32[64,4,64,64]{3,2,1,0:T(8,128)} copy(f32[64,4,64,64]{3,2,0,1:T(8,128)S(1)} %convolution_bitcast_fusion) | data formatting | bytes 8388608 | tf_op jit(solution)/shard_map/vacs,ct->avst/transpose | solution.py:14
  46.6 6.9 %reshape.7 = f32[64,16384]{1,0:T(8,128)} reshape(f32[64,4,64,64]{3,2,1,0:T(8,128)} %copy.5) | data formatting | bytes 8388608 | tf_op jit(solution)/shard_map/reshape | solution.py:15
  53.5 0.0 reduce-scatter.2.cloned.1.call-update
  53.5 0.0 all-gather.2.cloned.1.call-start
  53.5 54.1 %reduce-scatter.2.cloned.1.call-done = f32[64,2048]{1,0:T(8,128)} async-done(((f32[64,16384]{1,0:T(8,128)}), f32[64,2048]{1,0:T(8,128)}) %reduce-scatter.2.cloned.1.call-update) | async-done | bytes 524304 | tf_op jit(solution)/shard_map/reduce_scatter | solution.py:16
  107.7 0.0 all-gather.2.cloned.1.call-update
  107.7 0.0 all-reduce.2.cloned.1.call-start
  107.7 48.1 %all-gather.2.cloned.1.call-done = f32[256,2048]{1,0:T(8,128)} async-done(((f32[64,2048]{1,0:T(8,128)}), f32[256,2048]{1,0:T(8,128)}) %all-gather.2.cloned.1.call-update) | async-done | bytes 2097168 | tf_op jit(solution)/shard_map/all_gather | solution.py:19
  155.9 4.4 %fusion.3 = f32[64,256]{1,0:T(8,128)} fusion(f32[64,2048]{1,0:T(8,128)} %reduce-scatter.2.cloned.1.call-done, f32[256,2048]{1,0:T(8,128)} %all-gather.2.cloned.1.call-done), kind=kOutput, calls=%fused_computation.5 | convolution fusion | flops 402653184 | bytes 2686976 | tf_op jit(solution)/shard_map/dot_general | solution.py:17
  160.3 0.0 all-reduce.2.cloned.1.call-update
  160.3 51.4 %all-reduce.2.cloned.1.call-done = f32[64,256]{1,0:T(8,128)} async-done(((f32[64,256]{1,0:T(8,128)}), f32[64,256]{1,0:T(8,128)}) %all-reduce.2.cloned.1.call-update) | async-done | bytes 65552 | tf_op jit(solution)/shard_map/psum | solution.py:23
  211.7 1.5 broadcast_multiply_fusion
Async XLA Ops:
  7.2 0.8 copy-start
  7.2 27.5 %copy-start.1 = (f32[64,64]{1,0:T(8,128)S(1)}, f32[64,64]{1,0:T(8,128)}, u32[]{:S(2)}) copy-start(f32[64,64]{1,0:T(8,128)} %param.5) | copy-start | bytes 49156
  7.2 100.5 %reduce-scatter.2.cloned.1.call-start = ((), (), s32[]{:S(2)}) async-start(), calls=%async_computation.1 | async-start | bytes 4718592 | tf_op jit(solution)/shard_map/reduce_scatter | solution.py:16
  53.5 102.4 %all-gather.2.cloned.1.call-start = ((), (), s32[]{:S(2)}) async-start(), calls=%async_computation.2 | async-start | bytes 2621440 | tf_op jit(solution)/shard_map/all_gather | solution.py:19
  107.7 104.0 %all-reduce.2.cloned.1.call-start = ((), (), s32[]{:S(2)}) async-start(), calls=%async_computation.3 | async-start | bytes 131072 | tf_op jit(solution)/shard_map/psum | solution.py:23
Sparse Core Ops, SparseCore 0:
  53.6 53.9 reduce-scatter.1
  109.9 45.9 all-gather.1
  160.4 51.1 all-reduce.1
where the time goes:
time: 220 us
  waiting for transfers between devices  154 us (70%)
  matrix products  38.9 us (18%)
  between operations  13.8 us (6%)
  local copies, waits for them, and re-layouts  11.8 us (5%)
    reduce_scatter x1, waiting for transfers between devices, body(): lax.psum_scatter(core, ('gy', 'gz'), scatter_dimension=1, tiled=True)  54.1 us
    psum x1, waiting for transfers between devices, body(): gram = lax.psum(partial_gram, ('gy', 'gz')) / jnp.float32(V * R * R)  51.4 us
    all_gather x1, waiting for transfers between devices, body(): lax.all_gather(projected, 'gx', axis=0, tiled=True)  48.1 us
    dot_general x1, matrix products, body(): first = jnp.einsum('vacb,bs->vacs', field, basis_two, precision=highest)  26.7 us
    dot_general x1, matrix products, body(): core = jnp.einsum('vacs,ct->avst', first, basis_three, precision=highest)  7.77 us
    reshape x1, local copies, waits for them, and re-layouts, body(): core = core.reshape(rows, -1)  6.91 us
    dot_general x1, matrix products, body(): jnp.dot(projected, lax.all_gather(projected, 'gx', axis=0, tiled=True).T,...  4.44 us
  transfers between devices with their start and end apart: 3, of which 3 were waited for; matrix products, arithmetic and copies ran while one was open for 0% of the time, Pallas kernels for 0%

commit v1 on v0

v1 whole, which is shorter than its diff:
```python
import functools

import jax
import jax.numpy as jnp
from jax import lax
from jax.experimental import pallas as pl
from jax.experimental.pallas import tpu as pltpu
from jax.sharding import PartitionSpec as P

MESH = pl.DeviceIdType.MESH
F32 = jnp.float32
BF16 = jnp.bfloat16
CHUNKS = 4
LANES = 128


def split(x):
    high = x.astype(BF16)
    return high, (x - high.astype(F32)).astype(BF16)


def mul(a, b):
    return lax.dot_general(a, b, (((1,), (0,)), ((), ())), preferred_element_type=F32)


def mul_t(a, b):
    return lax.dot_general(a, b, (((1,), (1,)), ((), ())), preferred_element_type=F32)


def kernel(shape, gsize, field, b2_ref, b3_ref, proj, gram, *scratch):
    (fbuf, w2, k3, k3f, core, rgz, half, rgy, xbuf, q1, q2, tbuf, t1, t2, gp, rg, fin,
     fsem, zs, zr, ys, yr, as_, ar, bs, br, ts, tr, gs, gr, hs, hr) = scratch
    nv, rows, depth, width = shape
    GX, GY, GZ = gsize
    rank = b2_ref.shape[1]
    tdim = b3_ref.shape[1]
    step = rows // CHUNKS
    pairs = step // 2
    sloc = rank // GZ
    cols = sloc * tdim
    nr = GY * GZ
    slab = rows // nr
    gx, gy, gz = lax.axis_index("gx"), lax.axis_index("gy"), lax.axis_index("gz")
    me = gy * GZ + gz

    def layer(d):
        other = lax.rem(me + d, nr)
        return other, (gx, other // GZ, lax.rem(other, GZ))

    loads = [
        pltpu.make_async_copy(
            field.at[:, pl.ds(k * step, step)], fbuf.at[:, pl.ds(k * step, step)], fsem.at[k]
        )
        for k in range(CHUNKS)
    ]
    for load in loads:
        load.start()

    barrier = pltpu.get_barrier_semaphore()
    for d in range(1, nr):
        pl.semaphore_signal(barrier, inc=1, device_id=layer(d)[1], device_id_type=MESH)
    for d in range(1, GX):
        pl.semaphore_signal(
            barrier, inc=1, device_id=(lax.rem(gx + d, GX), gy, gz), device_id_type=MESH
        )

    high, low = split(b2_ref[...].T)
    w2[0:rank, :] = high
    w2[rank : 2 * rank, :] = low
    k3f[...] = jnp.zeros_like(k3f)
    for i in range(4):
        k3f[i * depth : (i + 1) * depth, i * tdim : (i + 1) * tdim] = b3_ref[...]
    high, low = split(k3f[...])
    k3[0] = high
    k3[1] = low

    def contract(k):
        @pl.loop(0, pairs // 2)
        def _(j):
            base = k * step + 2 * j
            parts = []
            for v in range(nv):
                tile = jnp.concatenate(
                    [fbuf[v, base + o] for o in (0, pairs, 1, pairs + 1)], axis=0
                )
                high, low = split(tile)
                one = mul_t(w2[...], high)
                two = mul_t(w2[0:rank, :], low)
                parts.append(one[0:rank] + one[rank:] + two)
            high, low = split(jnp.concatenate(parts, axis=0))
            c = mul(high, k3[0]) + (mul(high, k3[1]) + mul(low, k3[0]))
            for z in range(GZ):
                for v in range(nv):
                    piece = c[v * rank + z * sloc : v * rank + (z + 1) * sloc]
                    core[k, z, v, 2 * j] = piece[:, 0:LANES]
                    core[k, z, v, 2 * j + 1] = piece[:, LANES:]

    def gz_copies(k):
        out = []
        for d in range(1, GZ):
            peer = lax.rem(gz + d, GZ)
            out.append(
                pltpu.make_async_remote_copy(
                    src_ref=core.at[k, peer], dst_ref=rgz.at[k, d - 1],
                    send_sem=zs.at[k, d - 1], recv_sem=zr.at[k, d - 1],
                    device_id=(gx, gy, peer), device_id_type=MESH,
                )
            )
        return out

    def gy_copies(k):
        out = []
        for d in range(1, GY):
            peer = lax.rem(gy + d, GY)
            out.append(
                pltpu.make_async_remote_copy(
                    src_ref=half.at[k, peer], dst_ref=rgy.at[k, d - 1],
                    send_sem=ys.at[k, d - 1], recv_sem=yr.at[k, d - 1],
                    device_id=(gx, peer, gz), device_id_type=MESH,
                )
            )
        return out

    upper = lax.rem(gx + 1, GX)
    across = lax.rem(gx + 2, GX)
    hcols = cols // 2
    sent = pl.multiple_of((across // 2) * hcols, LANES)
    mine = pl.multiple_of((gx // 2) * hcols, LANES)

    def gx_copies(k):
        r = pl.ds(k * step, step)
        return [
            pltpu.make_async_remote_copy(
                src_ref=proj.at[r], dst_ref=q1.at[r],
                send_sem=as_.at[k], recv_sem=ar.at[k],
                device_id=(upper, gy, gz), device_id_type=MESH,
            ),
            pltpu.make_async_remote_copy(
                src_ref=proj.at[r, pl.ds(sent, hcols)], dst_ref=q2.at[r],
                send_sem=bs.at[k], recv_sem=br.at[k],
                device_id=(across, gy, gz), device_id_type=MESH,
            ),
        ]

    zc = [gz_copies(k) for k in range(CHUNKS)]
    yc = [gy_copies(k) for k in range(CHUNKS)]
    xc = [gx_copies(k) for k in range(CHUNKS)]

    def stage_a(k):
        loads[k].wait()
        contract(k)
        if k == 0:
            pl.semaphore_wait(barrier, nr - 1 + GX - 1)
        for c in zc[k]:
            c.start()

    def stage_b(k):
        for c in zc[k]:
            c.wait_recv()

        @pl.loop(0, nv)
        def _(v):
            total = core[k, gz, v]
            for d in range(GZ - 1):
                total = total + rgz[k, d, v]
            half[k, v] = total

        for c in yc[k]:
            c.start()

    def stage_c(k):
        for c in yc[k]:
            c.wait_recv()
        total = half[k, gy]
        for d in range(GY - 1):
            total = total + rgy[k, d]
        xbuf[...] = total.reshape(pairs * sloc, LANES)
        lane = lax.broadcasted_iota(jnp.int32, (pairs, LANES), 1)
        first = lane < tdim
        for p in range(sloc // 2):
            a = xbuf[pl.ds(2 * p, pairs, stride=sloc), :]
            b = xbuf[pl.ds(2 * p + 1, pairs, stride=sloc), :]
            at = pl.ds(p * LANES, LANES)
            proj[pl.ds(k * step, pairs), at] = jnp.where(first, a, pltpu.roll(b, tdim, 1))
            proj[pl.ds(k * step + pairs, pairs), at] = jnp.where(
                first, pltpu.roll(a, tdim, 1), b
            )
        for c in xc[k]:
            c.start()

    stage_a(0)
    stage_a(1)
    stage_b(0)
    stage_a(2)
    stage_b(1)
    stage_a(3)
    stage_b(2)
    stage_b(3)
    for k in range(CHUNKS):
        stage_c(k)

    ph, pw = split(proj[...])
    hh, hw = split(proj[:, pl.ds(mine, hcols)])
    diag = mul_t(ph, ph) + (mul_t(ph, pw) + mul_t(pw, ph))
    for k in range(CHUNKS):
        for c in xc[k]:
            c.wait_recv()
    qh, qw = split(q1[...])
    n1 = mul_t(ph, qh) + (mul_t(ph, qw) + mul_t(pw, qh))
    n1t = mul_t(qh, ph) + (mul_t(qw, ph) + mul_t(qh, pw))
    qh, qw = split(q2[...])
    n2 = mul_t(hh, qh) + (mul_t(hh, qw) + mul_t(hw, qh))
    n2t = mul_t(qh, hh) + (mul_t(qw, hh) + mul_t(qh, hw))
    tbuf[...] = jnp.concatenate([n1t, n2t], axis=1)
    lower = lax.rem(gx + GX - 1, GX)
    swaps = [
        pltpu.make_async_remote_copy(
            src_ref=tbuf, dst_ref=t1, send_sem=ts.at[0], recv_sem=tr.at[0],
            device_id=(lower, gy, gz), device_id_type=MESH,
        ),
        pltpu.make_async_remote_copy(
            src_ref=tbuf, dst_ref=t2, send_sem=ts.at[1], recv_sem=tr.at[1],
            device_id=(across, gy, gz), device_id_type=MESH,
        ),
    ]
    for c in swaps:
        c.start()
    for c in swaps:
        c.wait_recv()
    r1 = t1[:, 0:rows]
    n2 = n2 + t2[:, rows:]
    blocks = []
    for j in range(GX):
        d = lax.rem(j - gx + GX, GX)
        blocks.append(
            jnp.where(d == 0, diag, jnp.where(d == 1, r1, jnp.where(d == 2, n2, n1)))
        )
    whole = jnp.concatenate(blocks, axis=1) * F32(1.0 / (nv * rank * tdim))
    for r in range(nr):
        gp[r] = whole[r * slab : (r + 1) * slab]
    gather = []
    for d in range(1, nr):
        other, where = layer(d)
        gather.append(
            pltpu.make_async_remote_copy(
                src_ref=gp.at[other], dst_ref=rg.at[d - 1],
                send_sem=gs.at[d - 1], recv_sem=gr.at[d - 1],
                device_id=where, device_id_type=MESH,
            )
        )
    for c in gather:
        c.start()
    for c in gather:
        c.wait_recv()
    total = gp[me]
    for d in range(nr - 1):
        total = total + rg[d]
    fin[me] = total
    spread = []
    for d in range(1, nr):
        other, where = layer(d)
        spread.append(
            pltpu.make_async_remote_copy(
                src_ref=fin.at[me], dst_ref=fin.at[me],
                send_sem=hs.at[d - 1], recv_sem=hr.at[d - 1],
                device_id=where, device_id_type=MESH,
            )
        )
    for c in spread:
        c.start()
    for c in spread:
        c.wait_recv()
    for r in range(nr):
        gram[r * slab : (r + 1) * slab, :] = fin[r]
    for group in zc + yc + xc + [swaps, gather, spread]:
        for c in group:
            c.wait_send()


def body(gsize, field, basis_two, basis_three):
    nv, rows, depth, width = field.shape
    rank, tdim = basis_two.shape[1], basis_three.shape[1]
    GX, GY, GZ = gsize
    assert GX == 4 and GY == nv and 4 * depth == 256 and 2 * tdim == LANES
    sloc = rank // GZ
    cols = sloc * tdim
    step = rows // CHUNKS
    pairs = step // 2
    nr = GY * GZ
    slab = rows // nr
    dma = pltpu.SemaphoreType.DMA
    vmem = pl.BlockSpec(memory_space=pltpu.VMEM)
    return pl.pallas_call(
        functools.partial(kernel, field.shape, gsize),
        out_shape=(
            jax.ShapeDtypeStruct((rows, cols), F32),
            jax.ShapeDtypeStruct((rows, GX * rows), F32),
        ),
        in_specs=[pl.BlockSpec(memory_space=pl.ANY), vmem, vmem],
        out_specs=(vmem, vmem),
        scratch_shapes=[
            pltpu.VMEM(field.shape, F32),
            pltpu.VMEM((2 * rank, width), BF16),
            pltpu.VMEM((2, 4 * depth, 4 * tdim), BF16),
            pltpu.VMEM((4 * depth, 4 * tdim), F32),
            pltpu.VMEM((CHUNKS, GZ, nv, pairs, sloc, LANES), F32),
            pltpu.VMEM((CHUNKS, GZ - 1, nv, pairs, sloc, LANES), F32),
            pltpu.VMEM((CHUNKS, nv, pairs, sloc, LANES), F32),
            pltpu.VMEM((CHUNKS, GY - 1, pairs, sloc, LANES), F32),
            pltpu.VMEM((pairs * sloc, LANES), F32),
            pltpu.VMEM((rows, cols), F32),
            pltpu.VMEM((rows, cols // 2), F32),
            pltpu.VMEM((rows, 2 * rows), F32),
            pltpu.VMEM((rows, 2 * rows), F32),
            pltpu.VMEM((rows, 2 * rows), F32),
            pltpu.VMEM((nr, slab, GX * rows), F32),
            pltpu.VMEM((nr - 1, slab, GX * rows), F32),
            pltpu.VMEM((nr, slab, GX * rows), F32),
            dma((CHUNKS,)),
            dma((CHUNKS, GZ - 1)),
            dma((CHUNKS, GZ - 1)),
            dma((CHUNKS, GY - 1)),
            dma((CHUNKS, GY - 1)),
            dma((CHUNKS,)),
            dma((CHUNKS,)),
            dma((CHUNKS,)),
            dma((CHUNKS,)),
            dma((2,)),
            dma((2,)),
            dma((nr - 1,)),
            dma((nr - 1,)),
            dma((nr - 1,)),
            dma((nr - 1,)),
        ],
        compiler_params=pltpu.CompilerParams(
            collective_id=0, has_side_effects=True, vmem_limit_bytes=56 * 2**20
        ),
    )(field, basis_two, basis_three)


def solution(mesh):
    placed = (P(None, "gx", "gz", "gy"), P("gy", None), P("gz", None))
    gsize = tuple(mesh.shape[name] for name in ("gx", "gy", "gz"))
    return jax.shard_map(
        functools.partial(body, gsize),
        mesh=mesh,
        in_specs=placed,
        out_specs=(P("gx", ("gy", "gz")), P("gx", None)),
        check_vma=False,
    )
```

time: 220 us -> 61.9 us (0.28)
  waiting for transfers between devices: 154 us -> 0 us
  Pallas kernels: 0 us -> 55.9 us
  matrix products: 38.9 us -> 0 us
  between operations: 13.8 us -> 0.64 us
  local copies, waits for them, and re-layouts: 11.8 us -> 4.94 us
    pallas_call x0 -> x1, Pallas kernels: none -> 55.9 us  [body(): pl.pallas_call(functools.partial(kernel, field.shape, gsize), out_shape=(...]
    reduce_scatter x1 -> x0, waiting for transfers between devices: 54.1 us -> none  [body(): lax.psum_scatter(core, ('gy', 'gz'), scatter_dimension=1, tiled=True)]
    psum x1 -> x0, waiting for transfers between devices: 51.4 us -> none  [body(): gram = lax.psum(partial_gram, ('gy', 'gz')) / jnp.float32(V * R * R)]
    all_gather x1 -> x0, waiting for transfers between devices: 48.1 us -> none  [body(): lax.all_gather(projected, 'gx', axis=0, tiled=True)]
    dot_general x3 -> x0, matrix products: 38.9 us -> none  [the longest x1 26.7 us: body(): first = jnp.einsum('vacb,bs->vacs', field, basis_two, precision=highest)]
    reshape x1 -> x0, local copies, waits for them, and re-layouts: 6.91 us -> none  [body(): core = core.reshape(rows, -1)]
    unnamed x4 -> x3, local copies, waits for them, and re-layouts: 0.79 us -> 4.94 us
    transpose x1 -> x0, local copies, waits for them, and re-layouts: 4.08 us -> none  [body(): core = jnp.einsum('vacs,ct->avst', first, basis_three, precision=highest)]
  transfers between devices with their start and end apart: 3 -> 0, of which waited for: 3 -> 0; matrix products, arithmetic and copies ran while one was open for 0% -> 0% of each run, Pallas kernels for 0% -> 0%
where the time goes in v1:
time: 61.9 us; the launch traced here: 61.5 us
  Pallas kernels  55.9 us (90%)
  local copies, waits for them, and re-layouts  4.94 us (8%)
  between operations  0.64 us (1%)
    pallas_call x1, Pallas kernels, body(): pl.pallas_call(functools.partial(kernel, field.shape, gsize), out_shape=(...  55.9 us
    unnamed x3, local copies, waits for them, and re-layouts  4.94 us

profile of v1, /device:TPU:0, one launch (start us, length us, event | category | flops | bytes accessed | tf_op | source)
XLA Modules:
  0.0 61.5 jit_solution(1919823723686636539)
XLA Ops:
  0.6 1.6 %copy.5.b2_ref = f32[256,64]{1,0:T(8,128)} copy(f32[256,64]{0,1:T(8,128)} %param.4) | data formatting | bytes 131072 | tf_op args[1]
  2.2 55.9 %shard_map.50 = (f32[64,2048]{1,0:T(8,128)}, f32[64,256]{1,0:T(8,128)}) custom-call(f32[4,64,64,256]{3,2,1,0:T(8,128)} %field.1, f32[256,64]{1,0:T(8,128)} %copy.5.b2_ref, f32[64,64]{1,0:T(8,128)} %b3_ref.1), custom_call_target="tpu_custom_call" | custom-call | tf_op jit(solution)/shard_map/pallas_call | solution.py:293
  58.2 1.9 %copy.8 = f32[64,2048]{1,0:T(8,128)} copy(f32[64,2048]{1,0:T(8,128)} %get-tuple-element.4) | data formatting | bytes 1048576
  60.0 1.5 %copy.9 = f32[64,256]{1,0:T(8,128)} copy(f32[64,256]{1,0:T(8,128)} %get-tuple-element.5) | data formatting | bytes 131072

commit v2 on v1

--- a/solution.py
+++ b/solution.py
@@ -10,7 +10,8 @@
 MESH = pl.DeviceIdType.MESH
 F32 = jnp.float32
 BF16 = jnp.bfloat16
-CHUNKS = 4
+CHUNKS = 8
+LAG = 3
 LANES = 128
 
 
@@ -32,7 +33,7 @@
      fsem, zs, zr, ys, yr, as_, ar, bs, br, ts, tr, gs, gr, hs, hr) = scratch
     nv, rows, depth, width = shape
     GX, GY, GZ = gsize
-    rank = b2_ref.shape[1]
+    rank = b2_ref.shape[0]
     tdim = b3_ref.shape[1]
     step = rows // CHUNKS
     pairs = step // 2
@@ -64,7 +65,7 @@
             barrier, inc=1, device_id=(lax.rem(gx + d, GX), gy, gz), device_id_type=MESH
         )
 
-    high, low = split(b2_ref[...].T)
+    high, low = split(b2_ref[...])
     w2[0:rank, :] = high
     w2[rank : 2 * rank, :] = low
     k3f[...] = jnp.zeros_like(k3f)
@@ -75,7 +76,7 @@
     k3[1] = low
 
     def contract(k):
-        @pl.loop(0, pairs // 2)
+        @pl.loop(0, pairs // 2, unroll=True)
         def _(j):
             base = k * step + 2 * j
             parts = []
@@ -188,16 +189,13 @@
         for c in xc[k]:
             c.start()
 
-    stage_a(0)
-    stage_a(1)
-    stage_b(0)
-    stage_a(2)
-    stage_b(1)
-    stage_a(3)
-    stage_b(2)
-    stage_b(3)
-    for k in range(CHUNKS):
-        stage_c(k)
+    for k in range(CHUNKS + LAG):
+        if k < CHUNKS:
+            stage_a(k)
+        if 1 <= k <= CHUNKS:
+            stage_b(k - 1)
+        if k >= LAG:
+            stage_c(k - LAG)
 
     ph, pw = split(proj[...])
     hh, hw = split(proj[:, pl.ds(mine, hcols)])
@@ -335,7 +333,7 @@
         compiler_params=pltpu.CompilerParams(
             collective_id=0, has_side_effects=True, vmem_limit_bytes=56 * 2**20
         ),
-    )(field, basis_two, basis_three)
+    )(field, basis_two.T, basis_three)
 
 
 def solution(mesh):

time: 61.9 us -> 55 us (0.89)
  Pallas kernels: 55.9 us -> 50.7 us
  local copies, waits for them, and re-layouts: 4.94 us -> 3.34 us
    pallas_call x1, Pallas kernels: 55.9 us -> 50.7 us  [body(): pl.pallas_call(functools.partial(kernel, field.shape, gsize), out_shape=(...]
    unnamed x3 -> x2, local copies, waits for them, and re-layouts: 4.94 us -> 3.34 us
where the time goes in v2:
time: 55 us; the launch traced here: 54.7 us
  Pallas kernels  50.7 us (92%)
  local copies, waits for them, and re-layouts  3.34 us (6%)
  between operations  0.64 us (1%)
    pallas_call x1, Pallas kernels, body(): pl.pallas_call(functools.partial(kernel, field.shape, gsize), out_shape=(...  50.7 us
    unnamed x2, local copies, waits for them, and re-layouts  3.34 us

profile of v2, /device:TPU:0, one launch (start us, length us, event | category | flops | bytes accessed | tf_op | source)
XLA Modules:
  0.0 54.7 jit_solution(5546575727956727887)
XLA Ops:
  0.6 50.7 %shard_map.50 = (f32[64,2048]{1,0:T(8,128)}, f32[64,256]{1,0:T(8,128)}) custom-call(f32[4,64,64,256]{3,2,1,0:T(8,128)} %field.1, f32[64,256]{1,0:T(8,128)} %bitcast.1, f32[64,64]{1,0:T(8,128)} %b3_ref.1), custom_call_target="tpu_custom_call" | custom-call | tf_op jit(solution)/shard_map/pallas_call | solution.py:291
  51.4 1.9 %copy.7 = f32[64,2048]{1,0:T(8,128)} copy(f32[64,2048]{1,0:T(8,128)} %get-tuple-element.4) | data formatting | bytes 1048576
  53.2 1.5 %copy.8 = f32[64,256]{1,0:T(8,128)} copy(f32[64,256]{1,0:T(8,128)} %get-tuple-element.5) | data formatting | bytes 131072

commit v3 on v2

--- a/solution.py
+++ b/solution.py
@@ -29,7 +29,7 @@
 
 
 def kernel(shape, gsize, field, b2_ref, b3_ref, proj, gram, *scratch):
-    (fbuf, w2, k3, k3f, core, rgz, half, rgy, xbuf, q1, q2, tbuf, t1, t2, gp, rg, fin,
+    (fbuf, w2f, w2, k3, k3f, core, rgz, half, rgy, xbuf, q1, q2, tbuf, t1, t2, gp, rg, fin,
      fsem, zs, zr, ys, yr, as_, ar, bs, br, ts, tr, gs, gr, hs, hr) = scratch
     nv, rows, depth, width = shape
     GX, GY, GZ = gsize
@@ -65,36 +65,45 @@
             barrier, inc=1, device_id=(lax.rem(gx + d, GX), gy, gz), device_id_type=MESH
         )
 
-    high, low = split(b2_ref[...])
-    w2[0:rank, :] = high
-    w2[rank : 2 * rank, :] = low
+    turned = b2_ref[...].T
+    w2f[...] = jnp.zeros_like(w2f)
+    for z in range(GZ):
+        for v in range(nv):
+            at = (z * nv + v) * sloc
+            w2f[v * width : (v + 1) * width, at : at + sloc] = turned[
+                :, z * sloc : (z + 1) * sloc
+            ]
+    high, low = split(w2f[...])
+    w2[0] = high
+    w2[1] = low
     k3f[...] = jnp.zeros_like(k3f)
+    turned = b3_ref[...].T
     for i in range(4):
-        k3f[i * depth : (i + 1) * depth, i * tdim : (i + 1) * tdim] = b3_ref[...]
+        k3f[i * tdim : (i + 1) * tdim, i * depth : (i + 1) * depth] = turned
     high, low = split(k3f[...])
-    k3[0] = high
-    k3[1] = low
+    k3[0 : 4 * tdim] = high
+    k3[4 * tdim :] = low
 
     def contract(k):
-        @pl.loop(0, pairs // 2, unroll=True)
-        def _(j):
-            base = k * step + 2 * j
-            parts = []
-            for v in range(nv):
-                tile = jnp.concatenate(
-                    [fbuf[v, base + o] for o in (0, pairs, 1, pairs + 1)], axis=0
-                )
-                high, low = split(tile)
-                one = mul_t(w2[...], high)
-                two = mul_t(w2[0:rank, :], low)
-                parts.append(one[0:rank] + one[rank:] + two)
-            high, low = split(jnp.concatenate(parts, axis=0))
-            c = mul(high, k3[0]) + (mul(high, k3[1]) + mul(low, k3[0]))
+        parts = [
+            split(fbuf[v, k * step : (k + 1) * step].reshape(step * depth, width))
+            for v in range(nv)
+        ]
+        high = jnp.concatenate([h for h, _ in parts], axis=1)
+        low = jnp.concatenate([l for _, l in parts], axis=1)
+        first = mul(high, w2[0]) + (mul(high, w2[1]) + mul(low, w2[0]))
+        high, low = split(first)
+        for j in range(pairs // 2):
+            order = (2 * j, 2 * j + pairs, 2 * j + 1, 2 * j + 1 + pairs)
+            h = jnp.concatenate([high[a * depth : (a + 1) * depth] for a in order], axis=0)
+            l = jnp.concatenate([low[a * depth : (a + 1) * depth] for a in order], axis=0)
+            one = mul(k3[...], h)
+            two = mul(k3[0 : 4 * tdim], l)
+            c = one[0 : 4 * tdim] + (one[4 * tdim :] + two)
             for z in range(GZ):
-                for v in range(nv):
-                    piece = c[v * rank + z * sloc : v * rank + (z + 1) * sloc]
-                    core[k, z, v, 2 * j] = piece[:, 0:LANES]
-                    core[k, z, v, 2 * j + 1] = piece[:, LANES:]
+                core[k, z, j * 4 * tdim : (j + 1) * 4 * tdim] = c[
+                    :, z * nv * sloc : (z + 1) * nv * sloc
+                ]
 
     def gz_copies(k):
         out = []
@@ -159,12 +168,13 @@
         for c in zc[k]:
             c.wait_recv()
 
-        @pl.loop(0, nv)
-        def _(v):
-            total = core[k, gz, v]
-            for d in range(GZ - 1):
-                total = total + rgz[k, d, v]
-            half[k, v] = total
+        total = core[k, gz]
+        for d in range(GZ - 1):
+            total = total + rgz[k, d]
+        for q in range(pairs):
+            t = total[q * LANES : (q + 1) * LANES].T
+            for v in range(nv):
+                half[k, v, q] = t[v * sloc : (v + 1) * sloc]
 
         for c in yc[k]:
             c.start()
@@ -298,11 +308,12 @@
         out_specs=(vmem, vmem),
         scratch_shapes=[
             pltpu.VMEM(field.shape, F32),
-            pltpu.VMEM((2 * rank, width), BF16),
-            pltpu.VMEM((2, 4 * depth, 4 * tdim), BF16),
-            pltpu.VMEM((4 * depth, 4 * tdim), F32),
-            pltpu.VMEM((CHUNKS, GZ, nv, pairs, sloc, LANES), F32),
-            pltpu.VMEM((CHUNKS, GZ - 1, nv, pairs, sloc, LANES), F32),
+            pltpu.VMEM((nv * width, nv * rank), F32),
+            pltpu.VMEM((2, nv * width, nv * rank), BF16),
+            pltpu.VMEM((8 * tdim, 4 * depth), BF16),
+            pltpu.VMEM((4 * tdim, 4 * depth), F32),
+            pltpu.VMEM((CHUNKS, GZ, step * tdim, nv * sloc), F32),
+            pltpu.VMEM((CHUNKS, GZ - 1, step * tdim, nv * sloc), F32),
             pltpu.VMEM((CHUNKS, nv, pairs, sloc, LANES), F32),
             pltpu.VMEM((CHUNKS, GY - 1, pairs, sloc, LANES), F32),
             pltpu.VMEM((pairs * sloc, LANES), F32),

time: 55 us -> 56.5 us (1.027)
  Pallas kernels: 50.7 us -> 52.2 us
    pallas_call x1, Pallas kernels: 50.7 us -> 52.2 us  [body(): pl.pallas_call(functools.partial(kernel, field.shape, gsize), out_shape=(...]
where the time goes in v3:
time: 56.5 us; the launch traced here: 56.2 us
  Pallas kernels  52.2 us (92%)
  local copies, waits for them, and re-layouts  3.34 us (6%)
  between operations  0.64 us (1%)
    pallas_call x1, Pallas kernels, body(): pl.pallas_call(functools.partial(kernel, field.shape, gsize), out_shape=(...  52.2 us
    unnamed x2, local copies, waits for them, and re-layouts  3.34 us

profile of v3, /device:TPU:0, one launch (start us, length us, event | category | flops | bytes accessed | tf_op | source)
XLA Modules:
  0.0 56.2 jit_solution(2273604142694414506)
XLA Ops:
  0.6 52.2 %shard_map.50 = (f32[64,2048]{1,0:T(8,128)}, f32[64,256]{1,0:T(8,128)}) custom-call(f32[4,64,64,256]{3,2,1,0:T(8,128)} %field.1, f32[64,256]{1,0:T(8,128)} %bitcast.1, f32[64,64]{1,0:T(8,128)} %b3_ref.1), custom_call_target="tpu_custom_call" | custom-call | tf_op jit(solution)/shard_map/pallas_call | solution.py:301
  52.9 1.9 %copy.7 = f32[64,2048]{1,0:T(8,128)} copy(f32[64,2048]{1,0:T(8,128)} %get-tuple-element.4) | data formatting | bytes 1048576
  54.7 1.5 %copy.8 = f32[64,256]{1,0:T(8,128)} copy(f32[64,256]{1,0:T(8,128)} %get-tuple-element.5) | data formatting | bytes 131072

commit v4 on v3

--- a/solution.py
+++ b/solution.py
@@ -48,14 +48,15 @@
         other = lax.rem(me + d, nr)
         return other, (gx, other // GZ, lax.rem(other, GZ))
 
-    loads = [
-        pltpu.make_async_copy(
-            field.at[:, pl.ds(k * step, step)], fbuf.at[:, pl.ds(k * step, step)], fsem.at[k]
-        )
-        for k in range(CHUNKS)
-    ]
-    for load in loads:
-        load.start()
+    def rows_of(k):
+        return pl.ds(pl.multiple_of(k * step, step), step)
+
+    def load(k):
+        r = rows_of(k)
+        return pltpu.make_async_copy(field.at[:, r], fbuf.at[:, r], fsem.at[k])
+
+    for k in range(CHUNKS):
+        load(k).start()
 
     barrier = pltpu.get_barrier_semaphore()
     for d in range(1, nr):
@@ -86,7 +87,7 @@
 
     def contract(k):
         parts = [
-            split(fbuf[v, k * step : (k + 1) * step].reshape(step * depth, width))
+            split(fbuf[v, rows_of(k)].reshape(step * depth, width))
             for v in range(nv)
         ]
         high = jnp.concatenate([h for h, _ in parts], axis=1)
@@ -138,7 +139,7 @@
     mine = pl.multiple_of((gx // 2) * hcols, LANES)
 
     def gx_copies(k):
-        r = pl.ds(k * step, step)
+        r = rows_of(k)
         return [
             pltpu.make_async_remote_copy(
                 src_ref=proj.at[r], dst_ref=q1.at[r],
@@ -152,22 +153,20 @@
             ),
         ]
 
-    zc = [gz_copies(k) for k in range(CHUNKS)]
-    yc = [gy_copies(k) for k in range(CHUNKS)]
-    xc = [gx_copies(k) for k in range(CHUNKS)]
-
     def stage_a(k):
-        loads[k].wait()
+        load(k).wait()
         contract(k)
-        if k == 0:
+
+        @pl.when(k == 0)
+        def _():
             pl.semaphore_wait(barrier, nr - 1 + GX - 1)
-        for c in zc[k]:
+
+        for c in gz_copies(k):
             c.start()
 
     def stage_b(k):
-        for c in zc[k]:
+        for c in gz_copies(k):
             c.wait_recv()
-
         total = core[k, gz]
         for d in range(GZ - 1):
             total = total + rgz[k, d]
@@ -175,12 +174,11 @@
             t = total[q * LANES : (q + 1) * LANES].T
             for v in range(nv):
                 half[k, v, q] = t[v * sloc : (v + 1) * sloc]
-
-        for c in yc[k]:
+        for c in gy_copies(k):
             c.start()
 
     def stage_c(k):
-        for c in yc[k]:
+        for c in gy_copies(k):
             c.wait_recv()
         total = half[k, gy]
         for d in range(GY - 1):
@@ -188,31 +186,46 @@
         xbuf[...] = total.reshape(pairs * sloc, LANES)
         lane = lax.broadcasted_iota(jnp.int32, (pairs, LANES), 1)
         first = lane < tdim
+        done = []
         for p in range(sloc // 2):
             a = xbuf[pl.ds(2 * p, pairs, stride=sloc), :]
             b = xbuf[pl.ds(2 * p + 1, pairs, stride=sloc), :]
-            at = pl.ds(p * LANES, LANES)
-            proj[pl.ds(k * step, pairs), at] = jnp.where(first, a, pltpu.roll(b, tdim, 1))
-            proj[pl.ds(k * step + pairs, pairs), at] = jnp.where(
-                first, pltpu.roll(a, tdim, 1), b
-            )
-        for c in xc[k]:
+            done.append(
+                jnp.concatenate(
+                    [
+                        jnp.where(first, a, pltpu.roll(b, tdim, 1)),
+                        jnp.where(first, pltpu.roll(a, tdim, 1), b),
+                    ],
+                    axis=0,
+                )
+            )
+        proj[rows_of(k), :] = jnp.concatenate(done, axis=1)
+        for c in gx_copies(k):
             c.start()
 
-    for k in range(CHUNKS + LAG):
-        if k < CHUNKS:
+    @pl.loop(0, CHUNKS + LAG)
+    def _(k):
+        @pl.when(k < CHUNKS)
+        def _():
             stage_a(k)
-        if 1 <= k <= CHUNKS:
+
+        @pl.when((k >= 1) & (k <= CHUNKS))
+        def _():
             stage_b(k - 1)
-        if k >= LAG:
+
+        @pl.when(k >= LAG)
+        def _():
             stage_c(k - LAG)
 
     ph, pw = split(proj[...])
     hh, hw = split(proj[:, pl.ds(mine, hcols)])
     diag = mul_t(ph, ph) + (mul_t(ph, pw) + mul_t(pw, ph))
-    for k in range(CHUNKS):
-        for c in xc[k]:
+
+    @pl.loop(0, CHUNKS)
+    def _(k):
+        for c in gx_copies(k):
             c.wait_recv()
+
     qh, qw = split(q1[...])
     n1 = mul_t(ph, qh) + (mul_t(ph, qw) + mul_t(pw, qh))
     n1t = mul_t(qh, ph) + (mul_t(qw, ph) + mul_t(qh, pw))
@@ -280,8 +293,12 @@
         c.wait_recv()
     for r in range(nr):
         gram[r * slab : (r + 1) * slab, :] = fin[r]
-    for group in zc + yc + xc + [swaps, gather, spread]:
-        for c in group:
+    for c in swaps + gather + spread:
+        c.wait_send()
+
+    @pl.loop(0, CHUNKS)
+    def _(k):
+        for c in gz_copies(k) + gy_copies(k) + gx_copies(k):
             c.wait_send()
 
 

time: 56.5 us -> 55.6 us (0.984)
  Pallas kernels: 52.2 us -> 51.3 us
    pallas_call x1, Pallas kernels: 52.2 us -> 51.3 us  [body(): pl.pallas_call(functools.partial(kernel, field.shape, gsize), out_shape=(...]
where the time goes in v4:
time: 55.6 us; the launch traced here: 55.3 us
  Pallas kernels  51.3 us (92%)
  local copies, waits for them, and re-layouts  3.34 us (6%)
  between operations  0.64 us (1%)
    pallas_call x1, Pallas kernels, body(): pl.pallas_call(functools.partial(kernel, field.shape, gsize), out_shape=(...  51.3 us
    unnamed x2, local copies, waits for them, and re-layouts  3.34 us

profile of v4, /device:TPU:0, one launch (start us, length us, event | category | flops | bytes accessed | tf_op | source)
XLA Modules:
  0.0 55.3 jit_solution(11316209211308280369)
XLA Ops:
  0.6 51.3 %shard_map.50 = (f32[64,2048]{1,0:T(8,128)}, f32[64,256]{1,0:T(8,128)}) custom-call(f32[4,64,64,256]{3,2,1,0:T(8,128)} %field.1, f32[64,256]{1,0:T(8,128)} %bitcast.1, f32[64,64]{1,0:T(8,128)} %b3_ref.1), custom_call_target="tpu_custom_call" | custom-call | tf_op jit(solution)/shard_map/pallas_call | solution.py:318
  52.0 1.9 %copy.7 = f32[64,2048]{1,0:T(8,128)} copy(f32[64,2048]{1,0:T(8,128)} %get-tuple-element.4) | data formatting | bytes 1048576
  53.9 1.5 %copy.8 = f32[64,256]{1,0:T(8,128)} copy(f32[64,256]{1,0:T(8,128)} %get-tuple-element.5) | data formatting | bytes 131072

commit v5 on v4

--- a/solution.py
+++ b/solution.py
@@ -11,7 +11,7 @@
 F32 = jnp.float32
 BF16 = jnp.bfloat16
 CHUNKS = 8
-LAG = 3
+LAGS = (1, 2, 4, 5, 6)
 LANES = 128
 
 
@@ -29,8 +29,9 @@
 
 
 def kernel(shape, gsize, field, b2_ref, b3_ref, proj, gram, *scratch):
-    (fbuf, w2f, w2, k3, k3f, core, rgz, half, rgy, xbuf, q1, q2, tbuf, t1, t2, gp, rg, fin,
-     fsem, zs, zr, ys, yr, as_, ar, bs, br, ts, tr, gs, gr, hs, hr) = scratch
+    (fbuf, w2f, w2, k3, k3f, core, rgz, pa, pb, ra, rb, sa, sb, xbuf, qo, qn, qf,
+     tbuf, tin, obuf, gp, rg, fin,
+     fsem, zs, zr, ys, yr, os_, or_, ns, nr_, fs, fr, g1s, g2s, ts, tr, gs, gr, hs, hr) = scratch
     nv, rows, depth, width = shape
     GX, GY, GZ = gsize
     rank = b2_ref.shape[0]
@@ -119,39 +120,57 @@
             )
         return out
 
-    def gy_copies(k):
-        out = []
-        for d in range(1, GY):
-            peer = lax.rem(gy + d, GY)
-            out.append(
-                pltpu.make_async_remote_copy(
-                    src_ref=half.at[k, peer], dst_ref=rgy.at[k, d - 1],
-                    send_sem=ys.at[k, d - 1], recv_sem=yr.at[k, d - 1],
-                    device_id=(gx, peer, gz), device_id_type=MESH,
-                )
-            )
-        return out
-
-    upper = lax.rem(gx + 1, GX)
-    across = lax.rem(gx + 2, GX)
+    def remote(src, dst, send, recv, where):
+        return pltpu.make_async_remote_copy(
+            src_ref=src, dst_ref=dst, send_sem=send, recv_sem=recv,
+            device_id=where, device_id_type=MESH,
+        )
+
+    y, x = gy // 2, lax.rem(gy, 2)
+    along_x = (gx, y * 2 + 1 - x, gz)
+    along_y = (gx, (1 - y) * 2 + x, gz)
+
+    def first_copies(k):
+        return [
+            remote(pa.at[k, 1 - x], ra.at[k], ys.at[k, 0], yr.at[k, 0], along_x),
+            remote(pb.at[k, 1 - y], rb.at[k], ys.at[k, 1], yr.at[k, 1], along_y),
+        ]
+
+    def second_copies(k):
+        return [
+            remote(pa.at[k, x, 1 - y], sa.at[k], ys.at[k, 2], yr.at[k, 2], along_y),
+            remote(pb.at[k, y, 1 - x], sb.at[k], ys.at[k, 3], yr.at[k, 3], along_x),
+        ]
+
+    side = gx // 2
+    inner = (gx == 1) | (gx == 2)
+    outer = jnp.logical_not(inner)
+    mate = gx + 1 - 2 * lax.rem(gx, 2)
+    far_inner, far_outer = 2 - side, 3 * (1 - side)
     hcols = cols // 2
-    sent = pl.multiple_of((across // 2) * hcols, LANES)
-    mine = pl.multiple_of((gx // 2) * hcols, LANES)
-
-    def gx_copies(k):
-        r = rows_of(k)
-        return [
-            pltpu.make_async_remote_copy(
-                src_ref=proj.at[r], dst_ref=q1.at[r],
-                send_sem=as_.at[k], recv_sem=ar.at[k],
-                device_id=(upper, gy, gz), device_id_type=MESH,
-            ),
-            pltpu.make_async_remote_copy(
-                src_ref=proj.at[r, pl.ds(sent, hcols)], dst_ref=q2.at[r],
-                send_sem=bs.at[k], recv_sem=br.at[k],
-                device_id=(across, gy, gz), device_id_type=MESH,
-            ),
-        ]
+    to_mate, over = (mate, gy, gz), (GX - 1 - gx, gy, gz)
+    out_cols = pl.ds(pl.multiple_of(side * hcols, LANES), hcols)
+    in_cols = pl.ds(pl.multiple_of((1 - side) * hcols, LANES), hcols)
+
+    def whole_copy(k):
+        r = rows_of(k)
+        return remote(proj.at[r], qo.at[r], os_.at[k], or_.at[k], to_mate)
+
+    def near_copy(k):
+        r = rows_of(k)
+        return remote(proj.at[r, out_cols], qn.at[r], ns.at[k], nr_.at[k], over)
+
+    def far_copy(k):
+        r = rows_of(k)
+        return remote(qo.at[r, out_cols], qf.at[r], fs.at[k], fr.at[k], over)
+
+    def near_on(k):
+        r = rows_of(k)
+        return remote(qn.at[r], qn.at[r], g1s.at[k], nr_.at[k], to_mate)
+
+    def far_on(k):
+        r = rows_of(k)
+        return remote(qf.at[r], qf.at[r], g2s.at[k], fr.at[k], to_mate)
 
     def stage_a(k):
         load(k).wait()
@@ -173,16 +192,26 @@
         for q in range(pairs):
             t = total[q * LANES : (q + 1) * LANES].T
             for v in range(nv):
-                half[k, v, q] = t[v * sloc : (v + 1) * sloc]
-        for c in gy_copies(k):
+                piece = t[v * sloc : (v + 1) * sloc]
+                if q < pairs // 2:
+                    pa[k, v % 2, v // 2, q] = piece
+                else:
+                    pb[k, v // 2, v % 2, q - pairs // 2] = piece
+        for c in first_copies(k):
             c.start()
 
     def stage_c(k):
-        for c in gy_copies(k):
+        for c in first_copies(k):
             c.wait_recv()
-        total = half[k, gy]
-        for d in range(GY - 1):
-            total = total + rgy[k, d]
+        pa[k, x] = pa[k, x] + ra[k]
+        pb[k, y] = pb[k, y] + rb[k]
+        for c in second_copies(k):
+            c.start()
+
+    def stage_d(k):
+        for c in second_copies(k):
+            c.wait_recv()
+        total = jnp.concatenate([pa[k, x, y] + sa[k], pb[k, y, x] + sb[k]], axis=0)
         xbuf[...] = total.reshape(pairs * sloc, LANES)
         lane = lax.broadcasted_iota(jnp.int32, (pairs, LANES), 1)
         first = lane < tdim
@@ -200,61 +229,88 @@
                 )
             )
         proj[rows_of(k), :] = jnp.concatenate(done, axis=1)
-        for c in gx_copies(k):
-            c.start()
-
-    @pl.loop(0, CHUNKS + LAG)
+
+        @pl.when(outer)
+        def _():
+            whole_copy(k).start()
+
+        @pl.when(inner)
+        def _():
+            near_copy(k).start()
+
+    def stage_e(k):
+        @pl.when(inner)
+        def _():
+            whole_copy(k).wait_recv()
+            far_copy(k).start()
+            near_copy(k).wait_recv()
+            near_on(k).start()
+
+    def stage_f(k):
+        @pl.when(inner)
+        def _():
+            far_copy(k).wait_recv()
+            far_on(k).start()
+
+    stages = [stage_a, stage_b, stage_c, stage_d, stage_e, stage_f]
+
+    @pl.loop(0, CHUNKS + LAGS[-1])
     def _(k):
-        @pl.when(k < CHUNKS)
-        def _():
-            stage_a(k)
-
-        @pl.when((k >= 1) & (k <= CHUNKS))
-        def _():
-            stage_b(k - 1)
-
-        @pl.when(k >= LAG)
-        def _():
-            stage_c(k - LAG)
+        for stage, lag in zip(stages, (0,) + LAGS):
+            pl.when((k >= lag) & (k < CHUNKS + lag))(functools.partial(stage, k - lag))
 
     ph, pw = split(proj[...])
-    hh, hw = split(proj[:, pl.ds(mine, hcols)])
+    hh, hw = split(proj[:, in_cols])
     diag = mul_t(ph, ph) + (mul_t(ph, pw) + mul_t(pw, ph))
 
-    @pl.loop(0, CHUNKS)
-    def _(k):
-        for c in gx_copies(k):
-            c.wait_recv()
-
-    qh, qw = split(q1[...])
-    n1 = mul_t(ph, qh) + (mul_t(ph, qw) + mul_t(pw, qh))
-    n1t = mul_t(qh, ph) + (mul_t(qw, ph) + mul_t(qh, pw))
-    qh, qw = split(q2[...])
-    n2 = mul_t(hh, qh) + (mul_t(hh, qw) + mul_t(hw, qh))
-    n2t = mul_t(qh, hh) + (mul_t(qw, hh) + mul_t(qh, hw))
-    tbuf[...] = jnp.concatenate([n1t, n2t], axis=1)
-    lower = lax.rem(gx + GX - 1, GX)
+    @pl.when(outer)
+    def _():
+        @pl.loop(0, CHUNKS)
+        def _(k):
+            near_on(k).wait_recv()
+            far_on(k).wait_recv()
+
+    def pair(ah, aw, bh, bw):
+        return mul_t(ah, bh) + (mul_t(ah, bw) + mul_t(aw, bh))
+
+    bh, bw = split(qn[...])
+    near = pair(hh, hw, bh, bw)
+    tbuf[0] = pair(bh, bw, hh, hw)
+    bh, bw = split(qf[...])
+    far = pair(hh, hw, bh, bw)
+    tbuf[1] = pair(bh, bw, hh, hw)
+    kind = 1 - inner.astype(jnp.int32)
     swaps = [
-        pltpu.make_async_remote_copy(
-            src_ref=tbuf, dst_ref=t1, send_sem=ts.at[0], recv_sem=tr.at[0],
-            device_id=(lower, gy, gz), device_id_type=MESH,
-        ),
-        pltpu.make_async_remote_copy(
-            src_ref=tbuf, dst_ref=t2, send_sem=ts.at[1], recv_sem=tr.at[1],
-            device_id=(across, gy, gz), device_id_type=MESH,
-        ),
+        remote(tbuf.at[0], tin.at[kind], ts.at[0], tr.at[kind], (far_inner, gy, gz)),
+        remote(tbuf.at[1], tin.at[kind], ts.at[1], tr.at[kind], (far_outer, gy, gz)),
     ]
+    back = remote(tbuf.at[2], obuf, ts.at[2], tr.at[2], to_mate)
     for c in swaps:
         c.start()
-    for c in swaps:
-        c.wait_recv()
-    r1 = t1[:, 0:rows]
-    n2 = n2 + t2[:, rows:]
+
+    @pl.when(inner)
+    def _():
+        oh, ow = split(qo[...])
+        tbuf[2] = pair(oh, ow, ph, pw)
+        back.start()
+        obuf[...] = pair(ph, pw, oh, ow)
+
+    @pl.when(outer)
+    def _():
+        back.wait_recv()
+
+    for i in range(2):
+        remote(tbuf.at[i], tin.at[i], ts.at[i], tr.at[i], to_mate).wait_recv()
+    near = near + tin[0]
+    far = far + tin[1]
+    beside = obuf[...]
     blocks = []
     for j in range(GX):
-        d = lax.rem(j - gx + GX, GX)
         blocks.append(
-            jnp.where(d == 0, diag, jnp.where(d == 1, r1, jnp.where(d == 2, n2, n1)))
+            jnp.where(
+                gx == j, diag,
+                jnp.where(mate == j, beside, jnp.where(far_inner == j, near, far)),
+            )
         )
     whole = jnp.concatenate(blocks, axis=1) * F32(1.0 / (nv * rank * tdim))
     for r in range(nr):
@@ -296,17 +352,30 @@
     for c in swaps + gather + spread:
         c.wait_send()
 
+    @pl.when(inner)
+    def _():
+        back.wait_send()
+
     @pl.loop(0, CHUNKS)
     def _(k):
-        for c in gz_copies(k) + gy_copies(k) + gx_copies(k):
+        for c in gz_copies(k) + first_copies(k) + second_copies(k):
             c.wait_send()
+
+        @pl.when(outer)
+        def _():
+            whole_copy(k).wait_send()
+
+        @pl.when(inner)
+        def _():
+            for c in (near_copy(k), far_copy(k), near_on(k), far_on(k)):
+                c.wait_send()
 
 
 def body(gsize, field, basis_two, basis_three):
     nv, rows, depth, width = field.shape
     rank, tdim = basis_two.shape[1], basis_three.shape[1]
     GX, GY, GZ = gsize
-    assert GX == 4 and GY == nv and 4 * depth == 256 and 2 * tdim == LANES
+    assert GX == 4 and GY == 4 and nv == 4 and 4 * depth == 256 and 2 * tdim == LANES
     sloc = rank // GZ
     cols = sloc * tdim
     step = rows // CHUNKS
@@ -331,28 +400,37 @@
             pltpu.VMEM((4 * tdim, 4 * depth), F32),
             pltpu.VMEM((CHUNKS, GZ, step * tdim, nv * sloc), F32),
             pltpu.VMEM((CHUNKS, GZ - 1, step * tdim, nv * sloc), F32),
-            pltpu.VMEM((CHUNKS, nv, pairs, sloc, LANES), F32),
-            pltpu.VMEM((CHUNKS, GY - 1, pairs, sloc, LANES), F32),
+            pltpu.VMEM((CHUNKS, 2, 2, pairs // 2, sloc, LANES), F32),
+            pltpu.VMEM((CHUNKS, 2, 2, pairs // 2, sloc, LANES), F32),
+            pltpu.VMEM((CHUNKS, 2, pairs // 2, sloc, LANES), F32),
+            pltpu.VMEM((CHUNKS, 2, pairs // 2, sloc, LANES), F32),
+            pltpu.VMEM((CHUNKS, pairs // 2, sloc, LANES), F32),
+            pltpu.VMEM((CHUNKS, pairs // 2, sloc, LANES), F32),
             pltpu.VMEM((pairs * sloc, LANES), F32),
             pltpu.VMEM((rows, cols), F32),
             pltpu.VMEM((rows, cols // 2), F32),
-            pltpu.VMEM((rows, 2 * rows), F32),
-            pltpu.VMEM((rows, 2 * rows), F32),
-            pltpu.VMEM((rows, 2 * rows), F32),
+            pltpu.VMEM((rows, cols // 2), F32),
+            pltpu.VMEM((3, rows, rows), F32),
+            pltpu.VMEM((2, rows, rows), F32),
+            pltpu.VMEM((rows, rows), F32),
             pltpu.VMEM((nr, slab, GX * rows), F32),
             pltpu.VMEM((nr - 1, slab, GX * rows), F32),
             pltpu.VMEM((nr, slab, GX * rows), F32),
             dma((CHUNKS,)),
             dma((CHUNKS, GZ - 1)),
             dma((CHUNKS, GZ - 1)),
-            dma((CHUNKS, GY - 1)),
-            dma((CHUNKS, GY - 1)),
-            dma((CHUNKS,)),
-            dma((CHUNKS,)),
-            dma((CHUNKS,)),
-            dma((CHUNKS,)),
-            dma((2,)),
-            dma((2,)),
+            dma((CHUNKS, 4)),
+            dma((CHUNKS, 4)),
+            dma((CHUNKS,)),
+            dma((CHUNKS,)),
+            dma((CHUNKS,)),
+            dma((CHUNKS,)),
+            dma((CHUNKS,)),
+            dma((CHUNKS,)),
+            dma((CHUNKS,)),
+            dma((CHUNKS,)),
+            dma((3,)),
+            dma((3,)),
             dma((nr - 1,)),
             dma((nr - 1,)),
             dma((nr - 1,)),

time: 55.6 us -> 62.2 us (1.12)
  Pallas kernels: 51.3 us -> 58 us
    pallas_call x1, Pallas kernels: 51.3 us -> 58 us  [body(): pl.pallas_call(functools.partial(kernel, field.shape, gsize), out_shape=(...]
where the time goes in v5:
time: 62.2 us; the launch traced here: 61.9 us
  Pallas kernels  58 us (93%)
  local copies, waits for them, and re-layouts  3.34 us (5%)
  between operations  0.64 us (1%)
    pallas_call x1, Pallas kernels, body(): pl.pallas_call(functools.partial(kernel, field.shape, gsize), out_shape=(...  58 us
    unnamed x2, local copies, waits for them, and re-layouts  3.34 us

profile of v5, /device:TPU:0, one launch (start us, length us, event | category | flops | bytes accessed | tf_op | source)
XLA Modules:
  0.0 61.9 jit_solution(6555160107632553531)
XLA Ops:
  0.6 58.0 %shard_map.50 = (f32[64,2048]{1,0:T(8,128)}, f32[64,256]{1,0:T(8,128)}) custom-call(f32[4,64,64,256]{3,2,1,0:T(8,128)} %field.1, f32[64,256]{1,0:T(8,128)} %bitcast.1, f32[64,64]{1,0:T(8,128)} %b3_ref.1), custom_call_target="tpu_custom_call" | custom-call | tf_op jit(solution)/shard_map/pallas_call | solution.py:387
  58.6 1.9 %copy.7 = f32[64,2048]{1,0:T(8,128)} copy(f32[64,2048]{1,0:T(8,128)} %get-tuple-element.4) | data formatting | bytes 1048576
  60.5 1.5 %copy.8 = f32[64,256]{1,0:T(8,128)} copy(f32[64,256]{1,0:T(8,128)} %get-tuple-element.5) | data formatting | bytes 131072

commit v6 on v4

--- a/solution.py
+++ b/solution.py
@@ -11,7 +11,8 @@
 F32 = jnp.float32
 BF16 = jnp.bfloat16
 CHUNKS = 8
-LAG = 3
+LAG_B = 2
+LAG = 6
 LANES = 128
 
 
@@ -209,30 +210,33 @@
         def _():
             stage_a(k)
 
-        @pl.when((k >= 1) & (k <= CHUNKS))
+        @pl.when((k >= LAG_B) & (k < CHUNKS + LAG_B))
         def _():
-            stage_b(k - 1)
+            stage_b(k - LAG_B)
 
         @pl.when(k >= LAG)
         def _():
             stage_c(k - LAG)
 
+    def pair(both, high, other):
+        h, l = split(other)
+        one = mul_t(both, h)
+        return one[0:rows] + (one[rows:] + mul_t(high, l))
+
     ph, pw = split(proj[...])
     hh, hw = split(proj[:, pl.ds(mine, hcols)])
-    diag = mul_t(ph, ph) + (mul_t(ph, pw) + mul_t(pw, ph))
+    both = jnp.concatenate([ph, pw], axis=0)
+    half_both = jnp.concatenate([hh, hw], axis=0)
+    diag = pair(both, ph, proj[...])
 
     @pl.loop(0, CHUNKS)
     def _(k):
         for c in gx_copies(k):
             c.wait_recv()
 
-    qh, qw = split(q1[...])
-    n1 = mul_t(ph, qh) + (mul_t(ph, qw) + mul_t(pw, qh))
-    n1t = mul_t(qh, ph) + (mul_t(qw, ph) + mul_t(qh, pw))
-    qh, qw = split(q2[...])
-    n2 = mul_t(hh, qh) + (mul_t(hh, qw) + mul_t(hw, qh))
-    n2t = mul_t(qh, hh) + (mul_t(qw, hh) + mul_t(qh, hw))
-    tbuf[...] = jnp.concatenate([n1t, n2t], axis=1)
+    n1 = pair(both, ph, q1[...])
+    n2 = pair(half_both, hh, q2[...])
+    tbuf[...] = jnp.concatenate([n1.T, n2.T], axis=1)
     lower = lax.rem(gx + GX - 1, GX)
     swaps = [
         pltpu.make_async_remote_copy(
@@ -302,6 +306,17 @@
             c.wait_send()
 
 
+def settle(proj_in, gram_in, proj, gram, sem):
+    copies = [
+        pltpu.make_async_copy(proj_in, proj, sem.at[0]),
+        pltpu.make_async_copy(gram_in, gram, sem.at[1]),
+    ]
+    for c in copies:
+        c.start()
+    for c in copies:
+        c.wait()
+
+
 def body(gsize, field, basis_two, basis_three):
     nv, rows, depth, width = field.shape
     rank, tdim = basis_two.shape[1], basis_three.shape[1]
@@ -315,7 +330,7 @@
     slab = rows // nr
     dma = pltpu.SemaphoreType.DMA
     vmem = pl.BlockSpec(memory_space=pltpu.VMEM)
-    return pl.pallas_call(
+    results = pl.pallas_call(
         functools.partial(kernel, field.shape, gsize),
         out_shape=(
             jax.ShapeDtypeStruct((rows, cols), F32),
@@ -362,6 +377,14 @@
             collective_id=0, has_side_effects=True, vmem_limit_bytes=56 * 2**20
         ),
     )(field, basis_two.T, basis_three)
+    anywhere = pl.BlockSpec(memory_space=pl.ANY)
+    return pl.pallas_call(
+        settle,
+        out_shape=tuple(jax.ShapeDtypeStruct(r.shape, r.dtype) for r in results),
+        in_specs=[anywhere, anywhere],
+        out_specs=(anywhere, anywhere),
+        scratch_shapes=[dma((2,))],
+    )(*results)
 
 
 def solution(mesh):

time: 55.6 us -> 74.4 us (1.34)
  Pallas kernels: 51.3 us -> 73.6 us
  local copies, waits for them, and re-layouts: 3.34 us -> 0 us
    pallas_call x0 -> x1, Pallas kernels: none -> 19 us  [body(): pl.pallas_call(settle, out_shape=tuple((jax.ShapeDtypeStruct(r.shape, r.d...]
    unnamed x2 -> x0, local copies, waits for them, and re-layouts: 3.34 us -> none
    pallas_call x1, Pallas kernels: 51.3 us -> 54.6 us  [body(): pl.pallas_call(functools.partial(kernel, field.shape, gsize), out_shape=(...]
where the time goes in v6:
time: 74.4 us; the launch traced here: 74.3 us
  Pallas kernels  73.6 us (99%)
    pallas_call x1, Pallas kernels, body(): pl.pallas_call(functools.partial(kernel, field.shape, gsize), out_shape=(...  54.6 us
    pallas_call x1, Pallas kernels, body(): pl.pallas_call(settle, out_shape=tuple((jax.ShapeDtypeStruct(r.shape, r.d...  19 us

profile of v6, /device:TPU:0, one launch (start us, length us, event | category | flops | bytes accessed | tf_op | source)
XLA Modules:
  0.0 74.3 jit_solution(16556497565101968071)
XLA Ops:
  0.6 54.6 %shard_map.50 = (f32[64,2048]{1,0:T(8,128)}, f32[64,256]{1,0:T(8,128)}) custom-call(f32[4,64,64,256]{3,2,1,0:T(8,128)} %field.1, f32[64,256]{1,0:T(8,128)} %bitcast.1, f32[64,64]{1,0:T(8,128)} %b3_ref.1), custom_call_target="tpu_custom_call" | custom-call | tf_op jit(solution)/shard_map/pallas_call | solution.py:333
  55.3 19.0 %shard_map.51 = (f32[64,2048]{1,0:T(8,128)}, f32[64,256]{1,0:T(8,128)}) custom-call(f32[64,2048]{1,0:T(8,128)} %get-tuple-element.4.proj_in, f32[64,256]{1,0:T(8,128)} %get-tuple-element.5.gram_in), custom_call_target="tpu_custom_call" | custom-call | tf_op jit(solution)/shard_map/pallas_call | solution.py:381

commit v7 on v6

--- a/solution.py
+++ b/solution.py
@@ -11,8 +11,8 @@
 F32 = jnp.float32
 BF16 = jnp.bfloat16
 CHUNKS = 8
-LAG_B = 2
-LAG = 6
+LAG_B = 1
+LAG = 2
 LANES = 128
 
 
@@ -52,12 +52,13 @@
     def rows_of(k):
         return pl.ds(pl.multiple_of(k * step, step), step)
 
-    def load(k):
+    def load(k, v):
         r = rows_of(k)
-        return pltpu.make_async_copy(field.at[:, r], fbuf.at[:, r], fsem.at[k])
+        return pltpu.make_async_copy(field.at[v, r], fbuf.at[v, r], fsem.at[k, v])
 
     for k in range(CHUNKS):
-        load(k).start()
+        for v in range(nv):
+            load(k, v).start()
 
     barrier = pltpu.get_barrier_semaphore()
     for d in range(1, nr):
@@ -155,7 +156,8 @@
         ]
 
     def stage_a(k):
-        load(k).wait()
+        for v in range(nv):
+            load(k, v).wait()
         contract(k)
 
         @pl.when(k == 0)
@@ -306,17 +308,6 @@
             c.wait_send()
 
 
-def settle(proj_in, gram_in, proj, gram, sem):
-    copies = [
-        pltpu.make_async_copy(proj_in, proj, sem.at[0]),
-        pltpu.make_async_copy(gram_in, gram, sem.at[1]),
-    ]
-    for c in copies:
-        c.start()
-    for c in copies:
-        c.wait()
-
-
 def body(gsize, field, basis_two, basis_three):
     nv, rows, depth, width = field.shape
     rank, tdim = basis_two.shape[1], basis_three.shape[1]
@@ -330,7 +321,7 @@
     slab = rows // nr
     dma = pltpu.SemaphoreType.DMA
     vmem = pl.BlockSpec(memory_space=pltpu.VMEM)
-    results = pl.pallas_call(
+    return pl.pallas_call(
         functools.partial(kernel, field.shape, gsize),
         out_shape=(
             jax.ShapeDtypeStruct((rows, cols), F32),
@@ -357,7 +348,7 @@
             pltpu.VMEM((nr, slab, GX * rows), F32),
             pltpu.VMEM((nr - 1, slab, GX * rows), F32),
             pltpu.VMEM((nr, slab, GX * rows), F32),
-            dma((CHUNKS,)),
+            dma((CHUNKS, nv)),
             dma((CHUNKS, GZ - 1)),
             dma((CHUNKS, GZ - 1)),
             dma((CHUNKS, GY - 1)),
@@ -377,14 +368,6 @@
             collective_id=0, has_side_effects=True, vmem_limit_bytes=56 * 2**20
         ),
     )(field, basis_two.T, basis_three)
-    anywhere = pl.BlockSpec(memory_space=pl.ANY)
-    return pl.pallas_call(
-        settle,
-        out_shape=tuple(jax.ShapeDtypeStruct(r.shape, r.dtype) for r in results),
-        in_specs=[anywhere, anywhere],
-        out_specs=(anywhere, anywhere),
-        scratch_shapes=[dma((2,))],
-    )(*results)
 
 
 def solution(mesh):

time: 74.4 us -> 60.1 us (0.81)
  Pallas kernels: 73.6 us -> 55.8 us
  local copies, waits for them, and re-layouts: 0 us -> 3.34 us
    pallas_call x1 -> x0, Pallas kernels: 19 us -> none  [body(): pl.pallas_call(settle, out_shape=tuple((jax.ShapeDtypeStruct(r.shape, r.d...]
    unnamed x0 -> x2, local copies, waits for them, and re-layouts: none -> 3.34 us
    pallas_call x1, Pallas kernels: 54.6 us -> 55.8 us  [body(): pl.pallas_call(functools.partial(kernel, field.shape, gsize), out_shape=(...]
where the time goes in v7:
time: 60.1 us; the launch traced here: 59.8 us
  Pallas kernels  55.8 us (93%)
  local copies, waits for them, and re-layouts  3.34 us (6%)
  between operations  0.64 us (1%)
    pallas_call x1, Pallas kernels, body(): pl.pallas_call(functools.partial(kernel, field.shape, gsize), out_shape=(...  55.8 us
    unnamed x2, local copies, waits for them, and re-layouts  3.34 us

profile of v7, /device:TPU:0, one launch (start us, length us, event | category | flops | bytes accessed | tf_op | source)
XLA Modules:
  0.0 59.8 jit_solution(10971203818399879711)
XLA Ops:
  0.6 55.8 %shard_map.50 = (f32[64,2048]{1,0:T(8,128)}, f32[64,256]{1,0:T(8,128)}) custom-call(f32[4,64,64,256]{3,2,1,0:T(8,128)} %field.1, f32[64,256]{1,0:T(8,128)} %bitcast.1, f32[64,64]{1,0:T(8,128)} %b3_ref.1), custom_call_target="tpu_custom_call" | custom-call | tf_op jit(solution)/shard_map/pallas_call | solution.py:324
  56.5 1.9 %copy.7 = f32[64,2048]{1,0:T(8,128)} copy(f32[64,2048]{1,0:T(8,128)} %get-tuple-element.4) | data formatting | bytes 1048576
  58.3 1.5 %copy.8 = f32[64,256]{1,0:T(8,128)} copy(f32[64,256]{1,0:T(8,128)} %get-tuple-element.5) | data formatting | bytes 131072

commit v8 on v2

--- a/solution.py
+++ b/solution.py
@@ -275,6 +275,11 @@
             c.wait_send()
 
 
+def settle(proj_in, gram_in, proj, gram):
+    proj[...] = proj_in[...]
+    gram[...] = gram_in[...]
+
+
 def body(gsize, field, basis_two, basis_three):
     nv, rows, depth, width = field.shape
     rank, tdim = basis_two.shape[1], basis_three.shape[1]
@@ -288,7 +293,7 @@
     slab = rows // nr
     dma = pltpu.SemaphoreType.DMA
     vmem = pl.BlockSpec(memory_space=pltpu.VMEM)
-    return pl.pallas_call(
+    results = pl.pallas_call(
         functools.partial(kernel, field.shape, gsize),
         out_shape=(
             jax.ShapeDtypeStruct((rows, cols), F32),
@@ -334,6 +339,12 @@
             collective_id=0, has_side_effects=True, vmem_limit_bytes=56 * 2**20
         ),
     )(field, basis_two.T, basis_three)
+    return pl.pallas_call(
+        settle,
+        out_shape=tuple(jax.ShapeDtypeStruct(r.shape, r.dtype) for r in results),
+        in_specs=[vmem, vmem],
+        out_specs=(vmem, vmem),
+    )(*results)
 
 
 def solution(mesh):

time: 55 us -> 53.4 us (0.971)
  local copies, waits for them, and re-layouts: 3.34 us -> 0 us
  Pallas kernels: 50.7 us -> 52.6 us
    unnamed x2 -> x0, local copies, waits for them, and re-layouts: 3.34 us -> none
    pallas_call x0 -> x1, Pallas kernels: none -> 1.88 us  [body(): pl.pallas_call(settle, out_shape=tuple((jax.ShapeDtypeStruct(r.shape, r.d...]
where the time goes in v8:
time: 53.4 us; the launch traced here: 53.3 us
  Pallas kernels  52.6 us (99%)
  between operations  0.64 us (1%)
    pallas_call x1, Pallas kernels, body(): pl.pallas_call(functools.partial(kernel, field.shape, gsize), out_shape=(...  50.7 us
    pallas_call x1, Pallas kernels, body(): pl.pallas_call(settle, out_shape=tuple((jax.ShapeDtypeStruct(r.shape, r.d...  1.88 us

profile of v8, /device:TPU:0, one launch (start us, length us, event | category | flops | bytes accessed | tf_op | source)
XLA Modules:
  0.0 53.3 jit_solution(4177126561322714308)
XLA Ops:
  0.6 50.7 %shard_map.50 = (f32[64,2048]{1,0:T(8,128)}, f32[64,256]{1,0:T(8,128)}) custom-call(f32[4,64,64,256]{3,2,1,0:T(8,128)} %field.1, f32[64,256]{1,0:T(8,128)} %bitcast.1, f32[64,64]{1,0:T(8,128)} %b3_ref.1), custom_call_target="tpu_custom_call" | custom-call | tf_op jit(solution)/shard_map/pallas_call | solution.py:296
  51.4 1.9 %shard_map.51 = (f32[64,2048]{1,0:T(8,128)}, f32[64,256]{1,0:T(8,128)}) custom-call(f32[64,2048]{1,0:T(8,128)} %get-tuple-element.4.proj_in, f32[64,256]{1,0:T(8,128)} %get-tuple-element.5.gram_in), custom_call_target="tpu_custom_call" | custom-call | tf_op jit(solution)/shard_map/pallas_call | solution.py:342
